TPU v7x, 32 devices: a whole 2x2x4 slice. The times are simulated.
32 devices in a mesh: row: 8 (over y, x, core), col: 4 (over z).
Axes of the slice: x: 2, y: 2, z: 4, core: 2. Of those that a mesh axis runs over, the one named last changes fastest.
Arguments:
- integrals: bfloat16 [8192, 1024], P('row', 'col'), may hold values from -6 to 6
- amplitudes: bfloat16 [1024, 6144], P('row', 'col'), may hold values from -0.5 to 0.5
- screen: int32 [8, 48], P('row', 'col'), may hold values from 0 to 1, as said below
- next_owner: int32 [64], replicated, may hold values from 0 to 7, as said below
Outputs:
- regrouped: bfloat16 [8192, 6144], P('row', 'col')
Inputs may be any that keep to these rules, and one draw needn't show every extreme that they name: In each aligned block of 1 x 12 tiles of screen (one device's block), between 1 and 2 entries are 1; some block holds exactly 2. next_owner[p * 8 + s] equals p XOR m_s, where m_s (0 to 7) depends only on s.
All inputs are finite; a program needn't handle non-finite values.
Results may differ from a plain program's by a relative error of at most 0.001.
Values may be sent and summed in bfloat16 or wider, within the bound.
A program may use at most 128 MiB of HBM per device.

v0:
```python
import jax
import jax.numpy as jnp
from jax import lax
from jax.sharding import PartitionSpec as P

TILE = 128


def swapped(value, axis, bit):
    mask = 2**bit
    pairs = [(source, source ^ mask) for source in range(lax.axis_size(axis))]
    return lax.ppermute(value, axis, pairs)


def body(integrals, amplitudes, screen, next_owner):
    row_count = integrals.shape[0]
    depth_local = screen.shape[0]
    width_local = screen.shape[1]
    col_width = width_local * TILE
    rows_local = row_count // TILE
    moves = next_owner[:rows_local]
    bit_count = lax.axis_size("row").bit_length() - 1
    gathered = lax.all_gather(integrals, "col", axis=1, tiled=True)
    tile_flags = screen.astype(jnp.bfloat16)
    blocked = (
        amplitudes.reshape(depth_local, TILE, width_local, TILE) * tile_flags[:, None, :, None]
    )
    masked = blocked.reshape(depth_local * TILE, col_width)
    product = jnp.dot(
        gathered,
        lax.all_gather(masked, "row", axis=0, tiled=True),
        preferred_element_type=jnp.float32,
    )
    residual = product.astype(jnp.bfloat16)
    holding = residual.reshape(rows_local, TILE, col_width)
    for place_bit in range(bit_count):
        partner = swapped(holding, "row", place_bit)
        flipped = moves >> place_bit & 1 == 1
        holding = jnp.where(flipped[:, None, None], partner, holding)
    residual = holding.reshape(row_count, col_width)
    return residual


def solution(mesh):
    placed = (P("row", "col"), P("row", "col"), P("row", "col"), P())
    return jax.shard_map(
        body, mesh=mesh, in_specs=placed, out_specs=P("row", "col"), check_vma=False
    )
```

profile of v0, /device:TPU:0, one launch (start us, length us, event | category | flops | bytes accessed | tf_op | source)
XLA Modules:
  0.0 251.5 jit_solution(14931486623198799537)
XLA Ops:
  6.5 0.0 all-gather.5.cloned.1.call-start
  6.5 0.7 all-gather.5.cloned.1.call-update
  7.3 0.0 all-gather.3.cloned.1.call-start
  7.3 0.7 convert_bitcast_fusion
  8.0 0.1 broadcast_bitcast_fusion
  8.0 1.8 broadcast_multiply_fusion
  9.8 0.0 all-gather.3.cloned.1.call-update
  9.8 0.0 copy-start
  9.8 48.0 %all-gather.5.cloned.1.call-done = bf16[1024,1024]{1,0:T(8,128)(2,1)} async-done(((bf16[1024,256]{1,0:T(8,128)(2,1)}), bf16[1024,1024]{1,0:T(8,128)(2,1)}) %all-gather.5.cloned.1.call-update) | async-done | bytes 2097168 | tf_op jit(solution)/shard_map/all_gather | solution.py:23
  57.9 32.5 %all-gather.3.cloned.1.call-done = bf16[1024,1536]{1,0:T(8,128)(2,1)} async-done(((bf16[128,1536]{1,0:T(8,128)(2,1)}), bf16[1024,1536]{1,0:T(8,128)(2,1)}) %all-gather.3.cloned.1.call-update) | async-done | bytes 3145744 | tf_op jit(solution)/shard_map/all_gather | solution.py:31
  90.4 5.9 %convolution_convert_fusion = bf16[1536,1024]{0,1:T(8,128)(2,1)S(1)} fusion(bf16[1024,1024]{1,0:T(8,128)(2,1)} %all-gather.5.cloned.1.call-done, bf16[1024,1536]{1,0:T(8,128)(2,1)} %all-gather.3.cloned.1.call-done), kind=kOutput, calls=%fused_computation | convolution fusion | flops 3222798336 | bytes 8388608 | tf_op jit(solution)/shard_map/dot_general | solution.py:29
  96.3 0.3 collective-permute-start
  96.6 0.0 copy-done
  96.6 5.4 %collective-permute-done = bf16[8,128,1536]{2,1,0:T(8,128)(2,1)S(1)} collective-permute-done((bf16[8,128,1536]{2,1,0:T(8,128)(2,1)S(1)}, bf16[8,128,1536]{2,1,0:T(8,128)(2,1)S(1)}, u32[]{:S(2)}, u32[]{:S(2)}) %collective-permute-start) | collective-permute-done | bytes 3145760 | tf_op jit(solution)/shard_map/ppermute | solution.py:12
  102.0 0.4 broadcast_select_fusion
  102.4 1.5 collective-permute-start.1
  103.9 68.8 %collective-permute-done.1 = bf16[8,128,1536]{2,1,0:T(8,128)(2,1)S(1)} collective-permute-done((bf16[8,128,1536]{2,1,0:T(8,128)(2,1)S(1)}, bf16[8,128,1536]{2,1,0:T(8,128)(2,1)S(1)}, u32[]{:S(2)}, u32[]{:S(2)}) %collective-permute-start.1) | collective-permute-done | bytes 3145760 | tf_op jit(solution)/shard_map/ppermute | solution.py:12
  172.7 0.4 broadcast_select_fusion.1
  173.1 1.4 collective-permute-start.2
  174.5 68.1 %collective-permute-done.2 = bf16[8,128,1536]{2,1,0:T(8,128)(2,1)S(1)} collective-permute-done((bf16[8,128,1536]{2,1,0:T(8,128)(2,1)S(1)}, bf16[8,128,1536]{2,1,0:T(8,128)(2,1)S(1)}, u32[]{:S(2)}, u32[]{:S(2)}) %collective-permute-start.2) | collective-permute-done | bytes 3145760 | tf_op jit(solution)/shard_map/ppermute | solution.py:12
  242.6 2.0 broadcast_select_fusion.2
  (1 shorter events, 0.0 us)
Async XLA Ops:
  6.5 51.4 %all-gather.5.cloned.1.call-start = ((), (), s32[]{:S(2)}) async-start(), calls=%async_computation.1 | async-start | bytes 2621440 | tf_op jit(solution)/shard_map/all_gather | solution.py:23
  7.3 83.1 %all-gather.3.cloned.1.call-start = ((), (), s32[]{:S(2)}) async-start(), calls=%async_computation | async-start | bytes 3538944 | tf_op jit(solution)/shard_map/all_gather | solution.py:31
  9.8 86.8 %copy-start = (s32[64]{0:T(128)S(1)}, s32[64]{0:T(128)}, u32[]{:S(2)}) copy-start(s32[64]{0:T(128)} %param.7) | copy-start | bytes 772
  96.3 5.7 %collective-permute-start = (bf16[8,128,1536]{2,1,0:T(8,128)(2,1)S(1)}, bf16[8,128,1536]{2,1,0:T(8,128)(2,1)S(1)}, u32[]{:S(2)}, u32[]{:S(2)}) collective-permute-start(bf16[8,128,1536]{2,1,0:T(8,128)(2,1)S(1)} %bitcast.10), channel_id=1, source_target_pairs={{0,4},{4,0},{8,12},{12,8},{16,20},{20,16},{24,28},{28,24},{1,5},{5... | collective-permute-start | bytes 9437192 | tf_op jit(solution)/shard_map/ppermute | solution.py:12
  102.4 70.3 %collective-permute-start.1 = (bf16[8,128,1536]{2,1,0:T(8,128)(2,1)S(1)}, bf16[8,128,1536]{2,1,0:T(8,128)(2,1)S(1)}, u32[]{:S(2)}, u32[]{:S(2)}) collective-permute-start(bf16[8,128,1536]{2,1,0:T(8,128)(2,1)S(1)} %broadcast_select_fusion), channel_id=1, source_target_pairs={{0,8},{4,12},{8,0},{12,4},{16,24},{20,28},{24,16},{28,20},{1,9},{5... | collective-permute-start | bytes 9437192 | tf_op jit(solution)/shard_map/ppermute | solution.py:12
  173.1 69.5 %collective-permute-start.2 = (bf16[8,128,1536]{2,1,0:T(8,128)(2,1)S(1)}, bf16[8,128,1536]{2,1,0:T(8,128)(2,1)S(1)}, u32[]{:S(2)}, u32[]{:S(2)}) collective-permute-start(bf16[8,128,1536]{2,1,0:T(8,128)(2,1)S(1)} %broadcast_select_fusion.1), channel_id=1, source_target_pairs={{0,16},{4,20},{8,24},{12,28},{16,0},{20,4},{24,8},{28,12},{1,17},{... | collective-permute-start | bytes 9437192 | tf_op jit(solution)/shard_map/ppermute | solution.py:12
Sparse Core Ops, SparseCore 0:
  8.9 48.9 all-gather.4
  59.8 30.5 all-gather.2
where the time goes:
time: 252 us
  waiting for transfers between devices  224 us (89%)
  between operations  13.4 us (5%)
  matrix products  5.92 us (2%)
  other arithmetic  5.27 us (2%)
  starting transfers between devices  3.31 us (1%)
    ppermute x3, waiting for transfers between devices, swapped(): return lax.ppermute(value, axis, pairs)  142 us
    all_gather x1, waiting for transfers between devices, body(): gathered = lax.all_gather(integrals, 'col', axis=1, tiled=True)  48 us
    all_gather x1, waiting for transfers between devices, body(): lax.all_gather(masked, 'row', axis=0, tiled=True)  32.5 us
    dot_general x1, matrix products, body(): jnp.dot(gathered, lax.all_gather(masked, 'row', axis=0, tiled=True), pref...  5.92 us
  transfers between devices with their start and end apart: 5, of which 5 were waited for; matrix products, arithmetic and copies ran while one was open for 1% of the time, Pallas kernels for 0%

commit v1 on v0

v1 whole, which is shorter than its diff:
```python
import functools

import jax
import jax.numpy as jnp
from jax import lax
from jax.experimental import pallas as pl
from jax.experimental.pallas import tpu as pltpu
from jax.sharding import PartitionSpec as P

TILE = 128
CAP = 2
PAIR = 2
MESH = pl.DeviceIdType.MESH


def kernel(
    n_row, n_col, n_raw,
    a_ref, amp_ref, scr_ref, own_ref, out_ref,
    G, X, F, RX, AG, W, O,
    zr_send, zr_recv, zl_send, zl_recv, p_send, p_recv, r_send, r_recv, a_send, a_recv, o_sem,
):
    p = lax.axis_index("row")
    c = lax.axis_index("col")
    bits = n_row.bit_length() - 1
    tiles = a_ref.shape[0] // TILE
    width_tiles = amp_ref.shape[1] // TILE

    def partner(b):
        mask = 2**b
        return p + mask - 2 * mask * ((p // mask) % 2)

    barrier = pltpu.get_barrier_semaphore()
    for b in range(bits):
        pl.semaphore_signal(barrier, inc=1, device_id={"row": partner(b)}, device_id_type=MESH)

    @pl.when(c > 0)
    def _():
        pl.semaphore_signal(barrier, inc=1, device_id={"col": c - 1}, device_id_type=MESH)

    @pl.when(c < n_col - 1)
    def _():
        pl.semaphore_signal(barrier, inc=1, device_id={"col": c + 1}, device_id_type=MESH)

    near = (c > 0).astype(jnp.int32) + (c < n_col - 1).astype(jnp.int32)
    pl.semaphore_wait(barrier, bits + near)

    def rows(s):
        return pl.ds(s * TILE, TILE)

    def z_copy(s, h, right, block):
        src = a_ref.at[rows(s)] if h == 0 and s < n_raw else G.at[block, rows(s)]
        send, recv = (zr_send, zr_recv) if right else (zl_send, zl_recv)
        return pltpu.make_async_remote_copy(
            src_ref=src,
            dst_ref=G.at[block, rows(s)],
            send_sem=send.at[s, h],
            recv_sem=recv.at[s, h],
            device_id={"col": c + 1 if right else c - 1},
            device_id_type=MESH,
        )

    def z_wait(s, h):
        @pl.when(c - 1 - h >= 0)
        def _():
            z_copy(s, h, True, c - 1 - h).wait_recv()

        @pl.when(c + 1 + h < n_col)
        def _():
            z_copy(s, h, False, c + 1 + h).wait_recv()

    def z_edges(s, h, act):
        @pl.when((c - h >= 0) & (c < n_col - 1))
        def _():
            act(z_copy(s, h, True, c - h))

        @pl.when((c + h < n_col) & (c > 0))
        def _():
            act(z_copy(s, h, False, c + h))

    def z_hop(s, h):
        if h > 0:
            z_wait(s, h - 1)
        z_edges(s, h, lambda copy: copy.start())

    def order(s):
        far = list(range(1, bits))
        turn = s % len(far)
        return far[turn:] + far[:turn] + [0]

    def flip(s, b):
        return (own_ref[s] // 2**b) % 2 == 1

    def p_copy(s, i):
        b = order(s)[i]
        src = a_ref.at[rows(s)] if i == 0 else G.at[c, rows(s)]
        return pltpu.make_async_remote_copy(
            src_ref=src,
            dst_ref=X.at[i, rows(s - n_raw)],
            send_sem=p_send.at[s - n_raw, i],
            recv_sem=p_recv.at[s - n_raw, i],
            device_id={"row": partner(b)},
            device_id_type=MESH,
        )

    def p_stage(s, i):
        if i > 0:
            copy = p_copy(s, i - 1)
            copy.wait_recv()
            copy.wait_send()
            mine = a_ref[rows(s)] if i == 1 else G[c, rows(s)]
            G[c, rows(s)] = jnp.where(flip(s, order(s)[i - 1]), X[i - 1, rows(s - n_raw)], mine)
        if i < bits:
            p_copy(s, i).start()

    def r_copy(s, i):
        b = order(s)[i]
        src = G.at[:, rows(s)] if i == 0 else F.at[:, rows(s)]
        return pltpu.make_async_remote_copy(
            src_ref=src,
            dst_ref=RX.at[i, :, rows(s)],
            send_sem=r_send.at[s, i],
            recv_sem=r_recv.at[s, i],
            device_id={"row": partner(b)},
            device_id_type=MESH,
        )

    def r_stage(s, i):
        if i == 0:
            G[c, rows(s)] = a_ref[rows(s)]
        if i > 0:
            copy = r_copy(s, i - 1)
            copy.wait_recv()
            copy.wait_send()
            flipped = flip(s, order(s)[i - 1])
            for k in range(n_col):
                mine = G[k, rows(s)] if i == 1 else F[k, rows(s)]
                F[k, rows(s)] = jnp.where(flipped, RX[i - 1, k, rows(s)], mine)
        if i < bits:
            r_copy(s, i).start()

    def pack():
        count = jnp.int32(0)
        place = [jnp.int32(0)] * CAP
        for j in range(width_tiles):
            flag = scr_ref[0, j]
            for i in range(CAP):
                here = flag * (count == i).astype(jnp.int32)
                place[i] = place[i] + here * (j + 1)
            count = count + flag
        at = lax.broadcasted_iota(jnp.int32, (16, TILE), 0) + 1
        for i in range(CAP):
            total = jnp.zeros((TILE, TILE), jnp.float32)
            for j in range(width_tiles):
                block = amp_ref[:, j * TILE:(j + 1) * TILE].astype(jnp.float32)
                total = jnp.where(place[i] == j + 1, block, total)
            AG[p, i * TILE:(i + 1) * TILE] = total.astype(jnp.bfloat16)
            mark = jnp.where(at == place[i], 1.0, 0.0)
            AG[p, CAP * TILE + i * 16:CAP * TILE + (i + 1) * 16] = mark.astype(jnp.bfloat16)

    def a_copy(b):
        size = 2**b
        block = pl.ds((p // size) * size, size)
        return pltpu.make_async_remote_copy(
            src_ref=AG.at[block],
            dst_ref=AG.at[block],
            send_sem=a_send.at[b],
            recv_sem=a_recv.at[b],
            device_id={"row": partner(b)},
            device_id_type=MESH,
        )

    def a_wait(b):
        size = 2**b
        other = pl.ds((partner(b) // size) * size, size)
        pltpu.make_async_remote_copy(
            src_ref=AG.at[other],
            dst_ref=AG.at[other],
            send_sem=a_send.at[b],
            recv_sem=a_recv.at[b],
            device_id={"row": partner(b)},
            device_id_type=MESH,
        ).wait_recv()

    def expand():
        def step(k, carry):
            first = AG[k, 0:TILE].astype(jnp.float32)
            second = AG[k, TILE:2 * TILE].astype(jnp.float32)
            marks = AG[k, 2 * TILE:2 * TILE + 32].astype(jnp.float32)
            at = pl.ds(pl.multiple_of(k * TILE, TILE), TILE)
            for j in range(width_tiles):
                value = first * marks[j:j + 1] + second * marks[16 + j:17 + j]
                W[at, j * TILE:(j + 1) * TILE] = value.astype(jnp.bfloat16)
            return carry

        lax.fori_loop(0, n_row, step, 0)

    depth = a_ref.shape[1]
    wide = 2 * TILE

    def o_copy(q):
        at = pl.ds(q * PAIR * TILE, PAIR * TILE)
        return pltpu.make_async_copy(O.at[at], out_ref.at[at], o_sem.at[q])

    def compute(q):
        at = pl.ds(q * PAIR * TILE, PAIR * TILE)
        held = F if q * PAIR < n_raw else G

        def step(n, carry):
            cols = pl.ds(pl.multiple_of(n * wide, wide), wide)
            total = jnp.zeros((PAIR * TILE, wide), jnp.float32)
            for k in range(n_col):
                total += jnp.dot(
                    held[k, at], W[k * depth:(k + 1) * depth, cols], preferred_element_type=jnp.float32
                )
            O[at, cols] = total.astype(jnp.bfloat16)
            return carry

        lax.fori_loop(0, amp_ref.shape[1] // wide, step, 0)
        o_copy(q).start()

    pairs = tiles // PAIR
    raw_pairs = n_raw // PAIR

    def pair(q):
        return range(q * PAIR, (q + 1) * PAIR)

    last = n_col - 1
    slots = pairs + bits + n_col + bits + 4
    a_next = 0
    for slot in range(slots):
        for q in range(pairs):
            enter = q if q < raw_pairs else q - raw_pairs + bits
            if q >= raw_pairs:
                i = slot - (q - raw_pairs)
                if 0 <= i <= bits:
                    for s in pair(q):
                        p_stage(s, i)
            h = slot - enter
            if 0 <= h < last:
                for s in pair(q):
                    z_hop(s, h)
            if h == last:
                for s in pair(q):
                    z_wait(s, last - 1)
            if q < raw_pairs:
                i = slot - (enter + last + 1)
                if 0 <= i <= bits:
                    for s in pair(q):
                        r_stage(s, i)
        if slot == 0:
            pack()
            a_copy(0).start()
        elif slot <= bits:
            a_wait(slot - 1)
            if slot < bits:
                a_copy(slot).start()
            else:
                expand()
        for q in range(pairs):
            ready = q + last + 1 + bits if q < raw_pairs else q - raw_pairs + bits + last
            if slot == max(ready, bits):
                compute(q)

    for s in range(tiles):
        for h in range(last):
            z_edges(s, h, lambda copy: copy.wait_send())
    for b in range(bits):
        a_copy(b).wait_send()
    for q in range(pairs):
        o_copy(q).wait()


def body(integrals, amplitudes, screen, next_owner):
    n_row, n_col = lax.axis_size("row"), lax.axis_size("col")
    bits = n_row.bit_length() - 1
    row_count, depth = integrals.shape
    width = amplitudes.shape[1]
    tiles = row_count // TILE
    n_raw = PAIR
    late = row_count - n_raw * TILE
    last = n_col - 1
    dma = pltpu.SemaphoreType.DMA
    vmem = pl.BlockSpec(memory_space=pltpu.VMEM)
    smem = pl.BlockSpec(memory_space=pltpu.SMEM)
    bf16 = jnp.bfloat16
    return pl.pallas_call(
        functools.partial(kernel, n_row, n_col, n_raw),
        out_shape=jax.ShapeDtypeStruct((row_count, width), bf16),
        in_specs=[vmem, vmem, smem, smem],
        out_specs=pl.BlockSpec(memory_space=pl.ANY),
        scratch_shapes=[
            pltpu.VMEM((n_col, row_count, depth), bf16),
            pltpu.VMEM((bits, late, depth), bf16),
            pltpu.VMEM((n_col, n_raw * TILE, depth), bf16),
            pltpu.VMEM((bits, n_col, n_raw * TILE, depth), bf16),
            pltpu.VMEM((n_row, CAP * TILE + 32, TILE), bf16),
            pltpu.VMEM((n_row * TILE, width), bf16),
            pltpu.VMEM((row_count, width), bf16),
            dma((tiles, last)),
            dma((tiles, last)),
            dma((tiles, last)),
            dma((tiles, last)),
            dma((tiles - n_raw, bits)),
            dma((tiles - n_raw, bits)),
            dma((n_raw, bits)),
            dma((n_raw, bits)),
            dma((bits,)),
            dma((bits,)),
            dma((tiles // PAIR,)),
        ],
        compiler_params=pltpu.CompilerParams(
            collective_id=0, has_side_effects=True, vmem_limit_bytes=56 * 1024 * 1024
        ),
    )(integrals, amplitudes, screen, next_owner)


def solution(mesh):
    placed = (P("row", "col"), P("row", "col"), P("row", "col"), P())
    return jax.shard_map(
        body, mesh=mesh, in_specs=placed, out_specs=P("row", "col"), check_vma=False
    )
```

time: 252 us -> 60.3 us (0.24)
  waiting for transfers between devices: 224 us -> 0 us
  Pallas kernels: 0 us -> 56.4 us
  between operations: 13.4 us -> 0.01 us
  matrix products: 5.92 us -> 0 us
  other arithmetic: 5.27 us -> 0 us
  local copies, waits for them, and re-layouts: 0.08 us -> 3.76 us
  starting transfers between devices: 3.31 us -> 0 us
    ppermute x3 -> x0, waiting for transfers between devices: 142 us -> none  [swapped(): return lax.ppermute(value, axis, pairs)]
    all_gather x2 -> x0, waiting for transfers between devices: 80.5 us -> none  [the longest x1 48 us: body(): gathered = lax.all_gather(integrals, 'col', axis=1, tiled=True)]
    pallas_call x0 -> x1, Pallas kernels: none -> 56.4 us  [body(): pl.pallas_call(functools.partial(kernel, n_row, n_col, n_raw), out_shape=...]
    dot_general x1 -> x0, matrix products: 5.92 us -> none  [body(): jnp.dot(gathered, lax.all_gather(masked, 'row', axis=0, tiled=True), pref...]
    unnamed x2 -> x1, local copies, waits for them, and re-layouts: 0.01 us -> 3.76 us
    ppermute x3 -> x0, starting transfers between devices: 3.27 us -> none  [swapped(): return lax.ppermute(value, axis, pairs)]
    select_n x3 -> x0, other arithmetic: 2.82 us -> none  [body(): holding = jnp.where(flipped[:, None, None], partner, holding)]
  transfers between devices with their start and end apart: 5 -> 0, of which waited for: 5 -> 0; matrix products, arithmetic and copies ran while one was open for 1% -> 0% of each run, Pallas kernels for 0% -> 0%
where the time goes in v1:
time: 60.3 us; the launch traced here: 60.1 us
  Pallas kernels  56.4 us (94%)
  local copies, waits for them, and re-layouts  3.76 us (6%)
    pallas_call x1, Pallas kernels, body(): pl.pallas_call(functools.partial(kernel, n_row, n_col, n_raw), out_shape=...  56.4 us
    unnamed x1, local copies, waits for them, and re-layouts  3.76 us

profile of v1, /device:TPU:0, one launch (start us, length us, event | category | flops | bytes accessed | tf_op | source)
XLA Modules:
  0.0 60.1 jit_solution(7880947486934105280)
XLA Ops:
  0.0 56.4 %shard_map.46 = bf16[1024,1536]{1,0:T(8,128)(2,1)} custom-call(bf16[1024,256]{1,0:T(8,128)(2,1)} %a_ref.1, bf16[128,1536]{1,0:T(8,128)(2,1)} %amp_ref.1, s32[1,12]{1,0:T(1,128)} %scr_ref.1, s32[64]{0:T(128)} %own_ref.1), custom_call_target="tpu_custom_call" | custom-call | tf_op jit(solution)/shard_map/pallas_call | solution.py:286
  56.4 3.8 %copy.6 = bf16[1024,1536]{1,0:T(8,128)(2,1)} copy(bf16[1024,1536]{1,0:T(8,128)(2,1)} %shard_map.46) | data formatting | bytes 6291456

commit v2 on v1

--- a/solution.py
+++ b/solution.py
@@ -219,47 +219,54 @@
         o_copy(q).start()
 
     pairs = tiles // PAIR
-    raw_pairs = n_raw // PAIR
-
-    def pair(q):
-        return range(q * PAIR, (q + 1) * PAIR)
-
     last = n_col - 1
-    slots = pairs + bits + n_col + bits + 4
-    a_next = 0
-    for slot in range(slots):
-        for q in range(pairs):
-            enter = q if q < raw_pairs else q - raw_pairs + bits
-            if q >= raw_pairs:
-                i = slot - (q - raw_pairs)
-                if 0 <= i <= bits:
-                    for s in pair(q):
-                        p_stage(s, i)
-            h = slot - enter
-            if 0 <= h < last:
-                for s in pair(q):
-                    z_hop(s, h)
-            if h == last:
-                for s in pair(q):
-                    z_wait(s, last - 1)
-            if q < raw_pairs:
-                i = slot - (enter + last + 1)
-                if 0 <= i <= bits:
-                    for s in pair(q):
-                        r_stage(s, i)
-        if slot == 0:
+
+    steps = []
+
+    def at_place(place, step, *args):
+        steps.append((place, len(steps), step, args))
+
+    def own(s):
+        if s >= n_raw:
+            p_stage(s, bits)
+        z_hop(s, 0)
+
+    def a_stage(b):
+        if b > 0:
+            a_wait(b - 1)
+        if b == 0:
             pack()
-            a_copy(0).start()
-        elif slot <= bits:
-            a_wait(slot - 1)
-            if slot < bits:
-                a_copy(slot).start()
-            else:
-                expand()
-        for q in range(pairs):
-            ready = q + last + 1 + bits if q < raw_pairs else q - raw_pairs + bits + last
-            if slot == max(ready, bits):
-                compute(q)
+        if b < bits:
+            a_copy(b).start()
+        else:
+            expand()
+
+    shift = 0.6 * (bits - 3)
+    for s in range(tiles):
+        raw = s < n_raw
+        late = 0.0 if raw else shift
+        if raw:
+            at_place(0.0, own, s)
+        else:
+            at_place((1.6 + 0.01 * (s - n_raw) if s < n_raw + PAIR else s - 1.5) + late, own, s)
+            for i in range(bits):
+                at_place(0.05 + 0.6 * i + 0.65 * (s // PAIR - 1), p_stage, s, i)
+        for h in range(1, last):
+            place = 0.6 * h + 0.4 * s if raw else s + 0.4 + 0.8 * (h - 1)
+            at_place(place + late, z_hop, s, h)
+        at_place((2.3 + 0.5 * s if raw else s + 2.2) + late, z_wait, s, last - 1)
+        if raw:
+            for i in range(bits + 1):
+                at_place(2.85 + 1.7 * i - (0.9 if i == bits else 0.0), r_stage, s, i)
+    for b in range(bits + 1):
+        at_place(0.1 if b == 0 else 1.75 + 0.9 * (b - 1), a_stage, b)
+    for q in range(pairs):
+        if q * PAIR < n_raw:
+            at_place(2.0 + 1.7 * bits, compute, q)
+        else:
+            at_place(q * PAIR + 3.25 + shift, compute, q)
+    for place, index, step, args in sorted(steps, key=lambda entry: entry[:2]):
+        step(*args)
 
     for s in range(tiles):
         for h in range(last):

time: 60.3 us -> 63.2 us (1.048)
  Pallas kernels: 56.4 us -> 59.2 us
    pallas_call x1, Pallas kernels: 56.4 us -> 59.2 us  [body(): pl.pallas_call(functools.partial(kernel, n_row, n_col, n_raw), out_shape=...]
where the time goes in v2:
time: 63.2 us; the launch traced here: 63 us
  Pallas kernels  59.2 us (94%)
  local copies, waits for them, and re-layouts  3.76 us (6%)
    pallas_call x1, Pallas kernels, body(): pl.pallas_call(functools.partial(kernel, n_row, n_col, n_raw), out_shape=...  59.2 us
    unnamed x1, local copies, waits for them, and re-layouts  3.76 us

profile of v2, /device:TPU:0, one launch (start us, length us, event | category | flops | bytes accessed | tf_op | source)
XLA Modules:
  0.0 63.0 jit_solution(913089971896876773)
XLA Ops:
  0.0 59.2 %shard_map.46 = bf16[1024,1536]{1,0:T(8,128)(2,1)} custom-call(bf16[1024,256]{1,0:T(8,128)(2,1)} %a_ref.1, bf16[128,1536]{1,0:T(8,128)(2,1)} %amp_ref.1, s32[1,12]{1,0:T(1,128)} %scr_ref.1, s32[64]{0:T(128)} %own_ref.1), custom_call_target="tpu_custom_call" | custom-call | tf_op jit(solution)/shard_map/pallas_call | solution.py:293
  59.2 3.8 %copy.6 = bf16[1024,1536]{1,0:T(8,128)(2,1)} copy(bf16[1024,1536]{1,0:T(8,128)(2,1)} %shard_map.46) | data formatting | bytes 6291456

commit v3 on v2

--- a/solution.py
+++ b/solution.py
@@ -15,9 +15,9 @@
 
 def kernel(
     n_row, n_col, n_raw,
-    a_ref, amp_ref, scr_ref, own_ref, out_ref,
-    G, X, F, RX, AG, W, O,
-    zr_send, zr_recv, zl_send, zl_recv, p_send, p_recv, r_send, r_recv, a_send, a_recv, o_sem,
+    a_ref, amp_ref, scr_ref, own_ref, g_out, w_out,
+    G, X, F, RX, AG, W,
+    zr_send, zr_recv, zl_send, zl_recv, p_send, p_recv, r_send, r_recv, a_send, a_recv, g_sem, w_sem,
 ):
     p = lax.axis_index("row")
     c = lax.axis_index("col")
@@ -195,30 +195,19 @@
         lax.fori_loop(0, n_row, step, 0)
 
     depth = a_ref.shape[1]
-    wide = 2 * TILE
-
-    def o_copy(q):
-        at = pl.ds(q * PAIR * TILE, PAIR * TILE)
-        return pltpu.make_async_copy(O.at[at], out_ref.at[at], o_sem.at[q])
-
-    def compute(q):
-        at = pl.ds(q * PAIR * TILE, PAIR * TILE)
-        held = F if q * PAIR < n_raw else G
-
-        def step(n, carry):
-            cols = pl.ds(pl.multiple_of(n * wide, wide), wide)
-            total = jnp.zeros((PAIR * TILE, wide), jnp.float32)
-            for k in range(n_col):
-                total += jnp.dot(
-                    held[k, at], W[k * depth:(k + 1) * depth, cols], preferred_element_type=jnp.float32
-                )
-            O[at, cols] = total.astype(jnp.bfloat16)
-            return carry
-
-        lax.fori_loop(0, amp_ref.shape[1] // wide, step, 0)
-        o_copy(q).start()
-
-    pairs = tiles // PAIR
+
+    def g_copy(s, k):
+        held = F if s < n_raw else G
+        return pltpu.make_async_copy(
+            held.at[k, rows(s)], g_out.at[rows(s), pl.ds(k * depth, depth)], g_sem.at[s, k]
+        )
+
+    def put(s):
+        for k in range(n_col):
+            g_copy(s, k).start()
+
+    w_copy = pltpu.make_async_copy(W, w_out, w_sem.at[0])
+
     last = n_col - 1
 
     steps = []
@@ -240,6 +229,7 @@
             a_copy(b).start()
         else:
             expand()
+            w_copy.start()
 
     shift = 0.6 * (bits - 3)
     for s in range(tiles):
@@ -255,16 +245,12 @@
             place = 0.6 * h + 0.4 * s if raw else s + 0.4 + 0.8 * (h - 1)
             at_place(place + late, z_hop, s, h)
         at_place((2.3 + 0.5 * s if raw else s + 2.2) + late, z_wait, s, last - 1)
+        at_place((2.0 + 1.7 * bits if raw else s + 2.2) + late, put, s)
         if raw:
             for i in range(bits + 1):
                 at_place(2.85 + 1.7 * i - (0.9 if i == bits else 0.0), r_stage, s, i)
     for b in range(bits + 1):
         at_place(0.1 if b == 0 else 1.75 + 0.9 * (b - 1), a_stage, b)
-    for q in range(pairs):
-        if q * PAIR < n_raw:
-            at_place(2.0 + 1.7 * bits, compute, q)
-        else:
-            at_place(q * PAIR + 3.25 + shift, compute, q)
     for place, index, step, args in sorted(steps, key=lambda entry: entry[:2]):
         step(*args)
 
@@ -273,8 +259,10 @@
             z_edges(s, h, lambda copy: copy.wait_send())
     for b in range(bits):
         a_copy(b).wait_send()
-    for q in range(pairs):
-        o_copy(q).wait()
+    for s in range(tiles):
+        for k in range(n_col):
+            g_copy(s, k).wait()
+    w_copy.wait()
 
 
 def body(integrals, amplitudes, screen, next_owner):
@@ -290,11 +278,14 @@
     vmem = pl.BlockSpec(memory_space=pltpu.VMEM)
     smem = pl.BlockSpec(memory_space=pltpu.SMEM)
     bf16 = jnp.bfloat16
-    return pl.pallas_call(
+    gathered, screened = pl.pallas_call(
         functools.partial(kernel, n_row, n_col, n_raw),
-        out_shape=jax.ShapeDtypeStruct((row_count, width), bf16),
+        out_shape=[
+            jax.ShapeDtypeStruct((row_count, n_col * depth), bf16),
+            jax.ShapeDtypeStruct((n_row * TILE, width), bf16),
+        ],
         in_specs=[vmem, vmem, smem, smem],
-        out_specs=pl.BlockSpec(memory_space=pl.ANY),
+        out_specs=[pl.BlockSpec(memory_space=pl.ANY)] * 2,
         scratch_shapes=[
             pltpu.VMEM((n_col, row_count, depth), bf16),
             pltpu.VMEM((bits, late, depth), bf16),
@@ -302,7 +293,6 @@
             pltpu.VMEM((bits, n_col, n_raw * TILE, depth), bf16),
             pltpu.VMEM((n_row, CAP * TILE + 32, TILE), bf16),
             pltpu.VMEM((n_row * TILE, width), bf16),
-            pltpu.VMEM((row_count, width), bf16),
             dma((tiles, last)),
             dma((tiles, last)),
             dma((tiles, last)),
@@ -313,12 +303,14 @@
             dma((n_raw, bits)),
             dma((bits,)),
             dma((bits,)),
-            dma((tiles // PAIR,)),
+            dma((tiles, n_col)),
+            dma((1,)),
         ],
         compiler_params=pltpu.CompilerParams(
             collective_id=0, has_side_effects=True, vmem_limit_bytes=56 * 1024 * 1024
         ),
     )(integrals, amplitudes, screen, next_owner)
+    return jnp.dot(gathered, screened, preferred_element_type=jnp.float32).astype(bf16)
 
 
 def solution(mesh):

time: 63.2 us -> 62.3 us (0.986)
  matrix products: 0 us -> 7.59 us
  Pallas kernels: 59.2 us -> 54.6 us
  local copies, waits for them, and re-layouts: 3.76 us -> 0 us
    dot_general x0 -> x1, matrix products: none -> 7.59 us  [body(): jnp.dot(gathered, screened, preferred_element_type=jnp.float32).astype(bf16)]
    pallas_call x1, Pallas kernels: 59.2 us -> 54.6 us  [body(): pl.pallas_call(functools.partial(kernel, n_row, n_col, n_raw), out_shape=...]
    unnamed x1 -> x0, local copies, waits for them, and re-layouts: 3.76 us -> none
where the time goes in v3:
time: 62.3 us; the launch traced here: 62.2 us
  Pallas kernels  54.6 us (88%)
  matrix products  7.59 us (12%)
    pallas_call x1, Pallas kernels, body(): pl.pallas_call(functools.partial(kernel, n_row, n_col, n_raw), out_shape=...  54.6 us
    dot_general x1, matrix products, body(): jnp.dot(gathered, screened, preferred_element_type=jnp.float32).astype(bf16)  7.59 us

profile of v3, /device:TPU:0, one launch (start us, length us, event | category | flops | bytes accessed | tf_op | source)
XLA Modules:
  0.0 62.2 jit_solution(14051476414948785302)
XLA Ops:
  0.0 54.6 %shard_map.46 = (bf16[1024,1024]{1,0:T(8,128)(2,1)}, bf16[1024,1536]{1,0:T(8,128)(2,1)}) custom-call(bf16[1024,256]{1,0:T(8,128)(2,1)} %a_ref.1, bf16[128,1536]{1,0:T(8,128)(2,1)} %amp_ref.1, s32[1,12]{1,0:T(1,128)} %scr_ref.1, s32[64]{0:T(128)} %own_ref.1), custom_call_target="tpu_custom_call" | custom-call | tf_op jit(solution)/shard_map/pallas_call | solution.py:281
  54.6 7.6 %convolution_convert_fusion = bf16[1024,1536]{1,0:T(8,128)(2,1)} fusion(bf16[1024,1024]{1,0:T(8,128)(2,1)} %get-tuple-element.7, bf16[1024,1536]{1,0:T(8,128)(2,1)} %get-tuple-element.8), kind=kOutput, calls=%fused_computation | convolution fusion | flops 3222798336 | bytes 8388608 | tf_op jit(solution)/shard_map/dot_general | solution.py:313

commit v4 on v3

--- a/solution.py
+++ b/solution.py
@@ -10,6 +10,7 @@
 TILE = 128
 CAP = 2
 PAIR = 2
+LEAD = 2
 MESH = pl.DeviceIdType.MESH
 
 
@@ -238,14 +239,15 @@
         if raw:
             at_place(0.0, own, s)
         else:
-            at_place((1.6 + 0.01 * (s - n_raw) if s < n_raw + PAIR else s - 1.5) + late, own, s)
+            v = s - n_raw + LEAD
+            at_place((1.6 + 0.01 * (s - n_raw) if v < 2 * LEAD else v - 1.5) + late, own, s)
             for i in range(bits):
-                at_place(0.05 + 0.6 * i + 0.65 * (s // PAIR - 1), p_stage, s, i)
+                at_place(0.05 + 0.6 * i + 0.65 * ((s - n_raw) // PAIR), p_stage, s, i)
         for h in range(1, last):
-            place = 0.6 * h + 0.4 * s if raw else s + 0.4 + 0.8 * (h - 1)
+            place = 0.6 * h + 0.4 * s if raw else v + 0.4 + 0.8 * (h - 1)
             at_place(place + late, z_hop, s, h)
-        at_place((2.3 + 0.5 * s if raw else s + 2.2) + late, z_wait, s, last - 1)
-        at_place((2.0 + 1.7 * bits if raw else s + 2.2) + late, put, s)
+        at_place((2.3 + 0.5 * s if raw else v + 2.2) + late, z_wait, s, last - 1)
+        at_place((2.0 + 1.7 * bits if raw else v + 2.2) + late, put, s)
         if raw:
             for i in range(bits + 1):
                 at_place(2.85 + 1.7 * i - (0.9 if i == bits else 0.0), r_stage, s, i)
@@ -271,7 +273,7 @@
     row_count, depth = integrals.shape
     width = amplitudes.shape[1]
     tiles = row_count // TILE
-    n_raw = PAIR
+    n_raw = 0
     late = row_count - n_raw * TILE
     last = n_col - 1
     dma = pltpu.SemaphoreType.DMA
@@ -289,8 +291,8 @@
         scratch_shapes=[
             pltpu.VMEM((n_col, row_count, depth), bf16),
             pltpu.VMEM((bits, late, depth), bf16),
-            pltpu.VMEM((n_col, n_raw * TILE, depth), bf16),
-            pltpu.VMEM((bits, n_col, n_raw * TILE, depth), bf16),
+            pltpu.VMEM((n_col, max(n_raw, 1) * TILE, depth), bf16),
+            pltpu.VMEM((bits, n_col, max(n_raw, 1) * TILE, depth), bf16),
             pltpu.VMEM((n_row, CAP * TILE + 32, TILE), bf16),
             pltpu.VMEM((n_row * TILE, width), bf16),
             dma((tiles, last)),
@@ -299,8 +301,8 @@
             dma((tiles, last)),
             dma((tiles - n_raw, bits)),
             dma((tiles - n_raw, bits)),
-            dma((n_raw, bits)),
-            dma((n_raw, bits)),
+            dma((max(n_raw, 1), bits)),
+            dma((max(n_raw, 1), bits)),
             dma((bits,)),
             dma((bits,)),
             dma((tiles, n_col)),

time: 62.3 us -> 66.3 us (1.064)
  Pallas kernels: 54.6 us -> 58.6 us
    pallas_call x1, Pallas kernels: 54.6 us -> 58.6 us  [body(): pl.pallas_call(functools.partial(kernel, n_row, n_col, n_raw), out_shape=...]
where the time goes in v4:
time: 66.3 us; the launch traced here: 66.2 us
  Pallas kernels  58.6 us (88%)
  matrix products  7.6 us (11%)
    pallas_call x1, Pallas kernels, body(): pl.pallas_call(functools.partial(kernel, n_row, n_col, n_raw), out_shape=...  58.6 us
    dot_general x1, matrix products, body(): jnp.dot(gathered, screened, preferred_element_type=jnp.float32).astype(bf16)  7.6 us

profile of v4, /device:TPU:0, one launch (start us, length us, event | category | flops | bytes accessed | tf_op | source)
XLA Modules:
  0.0 66.2 jit_solution(11966671243525869459)
XLA Ops:
  0.0 58.6 %shard_map.46 = (bf16[1024,1024]{1,0:T(8,128)(2,1)}, bf16[1024,1536]{1,0:T(8,128)(2,1)}) custom-call(bf16[1024,256]{1,0:T(8,128)(2,1)} %a_ref.1, bf16[128,1536]{1,0:T(8,128)(2,1)} %amp_ref.1, s32[1,12]{1,0:T(1,128)} %scr_ref.1, s32[64]{0:T(128)} %own_ref.1), custom_call_target="tpu_custom_call" | custom-call | tf_op jit(solution)/shard_map/pallas_call | solution.py:283
  58.6 7.6 %convolution_convert_fusion = bf16[1024,1536]{1,0:T(8,128)(2,1)} fusion(bf16[1024,1024]{1,0:T(8,128)(2,1)} %get-tuple-element.7, bf16[1024,1536]{1,0:T(8,128)(2,1)} %get-tuple-element.8), kind=kOutput, calls=%fused_computation | convolution fusion | flops 3222798336 | bytes 8388608 | tf_op jit(solution)/shard_map/dot_general | solution.py:315

commit v5 on v3

--- a/solution.py
+++ b/solution.py
@@ -47,40 +47,41 @@
     def rows(s):
         return pl.ds(s * TILE, TILE)
 
-    def z_copy(s, h, right, block):
-        src = a_ref.at[rows(s)] if h == 0 and s < n_raw else G.at[block, rows(s)]
+    def z_copy(q, h, right, block):
+        at = pl.ds(q * PAIR * TILE, PAIR * TILE)
+        src = a_ref.at[at] if h == 0 and q * PAIR < n_raw else G.at[block, at]
         send, recv = (zr_send, zr_recv) if right else (zl_send, zl_recv)
         return pltpu.make_async_remote_copy(
             src_ref=src,
-            dst_ref=G.at[block, rows(s)],
-            send_sem=send.at[s, h],
-            recv_sem=recv.at[s, h],
+            dst_ref=G.at[block, at],
+            send_sem=send.at[q, h],
+            recv_sem=recv.at[q, h],
             device_id={"col": c + 1 if right else c - 1},
             device_id_type=MESH,
         )
 
-    def z_wait(s, h):
+    def z_wait(q, h):
         @pl.when(c - 1 - h >= 0)
         def _():
-            z_copy(s, h, True, c - 1 - h).wait_recv()
+            z_copy(q, h, True, c - 1 - h).wait_recv()
 
         @pl.when(c + 1 + h < n_col)
         def _():
-            z_copy(s, h, False, c + 1 + h).wait_recv()
-
-    def z_edges(s, h, act):
+            z_copy(q, h, False, c + 1 + h).wait_recv()
+
+    def z_edges(q, h, act):
         @pl.when((c - h >= 0) & (c < n_col - 1))
         def _():
-            act(z_copy(s, h, True, c - h))
+            act(z_copy(q, h, True, c - h))
 
         @pl.when((c + h < n_col) & (c > 0))
         def _():
-            act(z_copy(s, h, False, c + h))
-
-    def z_hop(s, h):
+            act(z_copy(q, h, False, c + h))
+
+    def z_hop(q, h):
         if h > 0:
-            z_wait(s, h - 1)
-        z_edges(s, h, lambda copy: copy.start())
+            z_wait(q, h - 1)
+        z_edges(q, h, lambda copy: copy.start())
 
     def order(s):
         far = list(range(1, bits))
@@ -209,16 +210,15 @@
     w_copy = pltpu.make_async_copy(W, w_out, w_sem.at[0])
 
     last = n_col - 1
+    pairs, raw_pairs = tiles // PAIR, n_raw // PAIR
+
+    def pair(q):
+        return range(q * PAIR, (q + 1) * PAIR)
 
     steps = []
 
     def at_place(place, step, *args):
         steps.append((place, len(steps), step, args))
-
-    def own(s):
-        if s >= n_raw:
-            p_stage(s, bits)
-        z_hop(s, 0)
 
     def a_stage(b):
         if b > 0:
@@ -231,38 +231,57 @@
             expand()
             w_copy.start()
 
+    def own(q):
+        if q >= raw_pairs:
+            for s in pair(q):
+                p_stage(s, bits)
+        z_hop(q, 0)
+
+    def put_pair(q):
+        for s in pair(q):
+            put(s)
+
     shift = 0.6 * (bits - 3)
-    for s in range(tiles):
-        raw = s < n_raw
-        late = 0.0 if raw else shift
-        if raw:
-            at_place(0.0, own, s)
+    for q in range(pairs):
+        j = q - raw_pairs
+        if q < raw_pairs:
+            at_place(0.0, own, q)
+            at_place(2.6, z_wait, q, last - 1)
+            at_place(2.2 + 1.7 * bits, put_pair, q)
         else:
-            at_place((1.6 + 0.01 * (s - n_raw) if s < n_raw + PAIR else s - 1.5) + late, own, s)
-            for i in range(bits):
-                at_place(0.05 + 0.6 * i + 0.65 * (s // PAIR - 1), p_stage, s, i)
+            at_place((1.6 if j == 0 else 1.0 + 1.2 * j) + shift, own, q)
+            at_place(4.4 + 1.5 * j + shift, z_wait, q, last - 1)
+            at_place(4.4 + 1.5 * j + shift, put_pair, q)
         for h in range(1, last):
-            place = 0.6 * h + 0.4 * s if raw else s + 0.4 + 0.8 * (h - 1)
-            at_place(place + late, z_hop, s, h)
-        at_place((2.3 + 0.5 * s if raw else s + 2.2) + late, z_wait, s, last - 1)
-        at_place((2.0 + 1.7 * bits if raw else s + 2.2) + late, put, s)
-        if raw:
+            if q < raw_pairs:
+                at_place(0.75 + 0.95 * (h - 1), z_hop, q, h)
+            else:
+                at_place(2.7 + 1.3 * j + (0.9 + 0.2 * j) * (h - 1) + shift, z_hop, q, h)
+        for s in pair(q):
             for i in range(bits + 1):
-                at_place(2.85 + 1.7 * i - (0.9 if i == bits else 0.0), r_stage, s, i)
+                if q < raw_pairs:
+                    at_place(2.65 + 1.7 * i - (0.9 if i == bits else 0.0), r_stage, s, i)
+                elif i < bits:
+                    at_place(0.05 + 0.6 * i + 0.65 * j, p_stage, s, i)
     for b in range(bits + 1):
         at_place(0.1 if b == 0 else 1.75 + 0.9 * (b - 1), a_stage, b)
     for place, index, step, args in sorted(steps, key=lambda entry: entry[:2]):
         step(*args)
 
-    for s in range(tiles):
+    for q in range(pairs):
         for h in range(last):
-            z_edges(s, h, lambda copy: copy.wait_send())
+            z_edges(q, h, lambda copy: copy.wait_send())
     for b in range(bits):
         a_copy(b).wait_send()
     for s in range(tiles):
         for k in range(n_col):
             g_copy(s, k).wait()
     w_copy.wait()
+
+
+def multiply(left_ref, right_ref, out_ref):
+    total = jnp.dot(left_ref[...], right_ref[...], preferred_element_type=jnp.float32)
+    out_ref[...] = total.astype(out_ref.dtype)
 
 
 def body(integrals, amplitudes, screen, next_owner):
@@ -293,10 +312,10 @@
             pltpu.VMEM((bits, n_col, n_raw * TILE, depth), bf16),
             pltpu.VMEM((n_row, CAP * TILE + 32, TILE), bf16),
             pltpu.VMEM((n_row * TILE, width), bf16),
-            dma((tiles, last)),
-            dma((tiles, last)),
-            dma((tiles, last)),
-            dma((tiles, last)),
+            dma((tiles // PAIR, last)),
+            dma((tiles // PAIR, last)),
+            dma((tiles // PAIR, last)),
+            dma((tiles // PAIR, last)),
             dma((tiles - n_raw, bits)),
             dma((tiles - n_raw, bits)),
             dma((n_raw, bits)),
@@ -310,7 +329,18 @@
             collective_id=0, has_side_effects=True, vmem_limit_bytes=56 * 1024 * 1024
         ),
     )(integrals, amplitudes, screen, next_owner)
-    return jnp.dot(gathered, screened, preferred_element_type=jnp.float32).astype(bf16)
+    wide = 2 * TILE
+    return pl.pallas_call(
+        multiply,
+        out_shape=jax.ShapeDtypeStruct((row_count, width), bf16),
+        grid=(width // wide,),
+        in_specs=[
+            pl.BlockSpec(gathered.shape, lambda n: (0, 0)),
+            pl.BlockSpec((screened.shape[0], wide), lambda n: (0, n)),
+        ],
+        out_specs=pl.BlockSpec((row_count, wide), lambda n: (0, n)),
+        compiler_params=pltpu.CompilerParams(vmem_limit_bytes=48 * 1024 * 1024),
+    )(gathered, screened)
 
 
 def solution(mesh):

time: 62.3 us -> 61 us (0.979)
  matrix products: 7.59 us -> 0 us
  local copies, waits for them, and re-layouts: 0 us -> 3.47 us
  Pallas kernels: 54.6 us -> 57.4 us
    dot_general x1 -> x0, matrix products: 7.59 us -> none  [body(): jnp.dot(gathered, screened, preferred_element_type=jnp.float32).astype(bf16)]
    pallas_call x0 -> x1, Pallas kernels: none -> 5.38 us  [body(): pl.pallas_call(multiply, out_shape=jax.ShapeDtypeStruct((row_count, width...]
    unnamed x0 -> x4, local copies, waits for them, and re-layouts: none -> 3.47 us
    pallas_call x1, Pallas kernels: 54.6 us -> 52 us  [body(): pl.pallas_call(functools.partial(kernel, n_row, n_col, n_raw), out_shape=...]
where the time goes in v5:
time: 61 us; the launch traced here: 60.8 us
  Pallas kernels  57.4 us (94%)
  local copies, waits for them, and re-layouts  3.47 us (6%)
    pallas_call x1, Pallas kernels, body(): pl.pallas_call(functools.partial(kernel, n_row, n_col, n_raw), out_shape=...  52 us
    pallas_call x1, Pallas kernels, body(): pl.pallas_call(multiply, out_shape=jax.ShapeDtypeStruct((row_count, width...  5.38 us
    unnamed x4, local copies, waits for them, and re-layouts  3.47 us

profile of v5, /device:TPU:0, one launch (start us, length us, event | category | flops | bytes accessed | tf_op | source)
XLA Modules:
  0.0 60.8 jit_solution(994306190064919528)
XLA Ops:
  0.0 52.0 %shard_map.46 = (bf16[1024,1024]{1,0:T(8,128)(2,1)}, bf16[1024,1536]{1,0:T(8,128)(2,1)}) custom-call(bf16[1024,256]{1,0:T(8,128)(2,1)} %a_ref.1, bf16[128,1536]{1,0:T(8,128)(2,1)} %amp_ref.1, s32[1,12]{1,0:T(1,128)} %scr_ref.1, s32[64]{0:T(128)} %own_ref.1), custom_call_target="tpu_custom_call" | custom-call | tf_op jit(solution)/shard_map/pallas_call | solution.py:300
  52.0 0.0 copy-start
  52.0 1.9 %copy-done = bf16[1024,1536]{1,0:T(8,128)(2,1)S(1)} copy-done((bf16[1024,1536]{1,0:T(8,128)(2,1)S(1)}, bf16[1024,1536]{1,0:T(8,128)(2,1)}, u32[]{:S(2)}) %copy-start) | copy-done | bytes 3145752
  53.9 0.0 copy-start.1
  53.9 1.6 %copy-done.1 = bf16[1024,1024]{1,0:T(8,128)(2,1)S(1)} copy-done((bf16[1024,1024]{1,0:T(8,128)(2,1)S(1)}, bf16[1024,1024]{1,0:T(8,128)(2,1)}, u32[]{:S(2)}) %copy-start.1) | copy-done | bytes 2097176
  55.5 5.4 %shard_map.47 = bf16[1024,1536]{1,0:T(8,128)(2,1)} custom-call(bf16[1024,1024]{1,0:T(8,128)(2,1)S(1)} %copy-done.1, bf16[1024,1536]{1,0:T(8,128)(2,1)S(1)} %copy-done), custom_call_target="tpu_custom_call" | custom-call | tf_op jit(solution)/shard_map/pallas_call | solution.py:333
Async XLA Ops:
  52.0 1.9 %copy-start = (bf16[1024,1536]{1,0:T(8,128)(2,1)S(1)}, bf16[1024,1536]{1,0:T(8,128)(2,1)}, u32[]{:S(2)}) copy-start(bf16[1024,1536]{1,0:T(8,128)(2,1)} %get-tuple-element.8.right_ref) | copy-start | bytes 9437188
  53.9 1.6 %copy-start.1 = (bf16[1024,1024]{1,0:T(8,128)(2,1)S(1)}, bf16[1024,1024]{1,0:T(8,128)(2,1)}, u32[]{:S(2)}) copy-start(bf16[1024,1024]{1,0:T(8,128)(2,1)} %get-tuple-element.7.left_ref) | copy-start | bytes 6291460

commit v6 on v5

--- a/solution.py
+++ b/solution.py
@@ -15,9 +15,9 @@
 
 def kernel(
     n_row, n_col, n_raw,
-    a_ref, amp_ref, scr_ref, own_ref, g_out, w_out,
-    G, X, F, RX, AG, W,
-    zr_send, zr_recv, zl_send, zl_recv, p_send, p_recv, r_send, r_recv, a_send, a_recv, g_sem, w_sem,
+    a_ref, amp_ref, scr_ref, own_ref, g_out, w_out, part_out,
+    G, X, F, RX, AG, W, O,
+    zr_send, zr_recv, zl_send, zl_recv, p_send, p_recv, r_send, r_recv, a_send, a_recv, g_sem, w_sem, o_sem,
 ):
     p = lax.axis_index("row")
     c = lax.axis_index("col")
@@ -197,15 +197,37 @@
 
     depth = a_ref.shape[1]
 
-    def g_copy(s, k):
-        held = F if s < n_raw else G
-        return pltpu.make_async_copy(
-            held.at[k, rows(s)], g_out.at[rows(s), pl.ds(k * depth, depth)], g_sem.at[s, k]
-        )
-
-    def put(s):
+    wide = 2 * TILE
+    kept = tiles // PAIR - 1
+
+    def g_copy(k):
+        at = pl.ds(kept * PAIR * TILE, PAIR * TILE)
+        return pltpu.make_async_copy(G.at[k, at], g_out.at[:, pl.ds(k * depth, depth)], g_sem.at[k])
+
+    def put(q):
         for k in range(n_col):
-            g_copy(s, k).start()
+            g_copy(k).start()
+
+    def o_copy(q):
+        at = pl.ds(q * PAIR * TILE, PAIR * TILE)
+        return pltpu.make_async_copy(O.at[at], part_out.at[at], o_sem.at[q])
+
+    def compute(q):
+        at = pl.ds(q * PAIR * TILE, PAIR * TILE)
+        held = F if q * PAIR < n_raw else G
+
+        def step(n, carry):
+            cols = pl.ds(pl.multiple_of(n * wide, wide), wide)
+            total = jnp.zeros((PAIR * TILE, wide), jnp.float32)
+            for k in range(n_col):
+                total += jnp.dot(
+                    held[k, at], W[k * depth:(k + 1) * depth, cols], preferred_element_type=jnp.float32
+                )
+            O[at, cols] = total.astype(jnp.bfloat16)
+            return carry
+
+        lax.fori_loop(0, amp_ref.shape[1] // wide, step, 0)
+        o_copy(q).start()
 
     w_copy = pltpu.make_async_copy(W, w_out, w_sem.at[0])
 
@@ -237,21 +259,20 @@
                 p_stage(s, bits)
         z_hop(q, 0)
 
-    def put_pair(q):
-        for s in pair(q):
-            put(s)
-
     shift = 0.6 * (bits - 3)
     for q in range(pairs):
         j = q - raw_pairs
         if q < raw_pairs:
             at_place(0.0, own, q)
             at_place(2.6, z_wait, q, last - 1)
-            at_place(2.2 + 1.7 * bits, put_pair, q)
+            at_place(6.9 + 1.7 * (bits - 3) + shift, compute, q)
         else:
             at_place((1.6 if j == 0 else 1.0 + 1.2 * j) + shift, own, q)
             at_place(4.4 + 1.5 * j + shift, z_wait, q, last - 1)
-            at_place(4.4 + 1.5 * j + shift, put_pair, q)
+            if q == kept:
+                at_place(4.4 + 1.5 * j + shift, put, q)
+            else:
+                at_place(5.35 + 1.6 * j + shift, compute, q)
         for h in range(1, last):
             if q < raw_pairs:
                 at_place(0.75 + 0.95 * (h - 1), z_hop, q, h)
@@ -273,15 +294,18 @@
             z_edges(q, h, lambda copy: copy.wait_send())
     for b in range(bits):
         a_copy(b).wait_send()
-    for s in range(tiles):
-        for k in range(n_col):
-            g_copy(s, k).wait()
+    for k in range(n_col):
+        g_copy(k).wait()
+    for q in range(kept):
+        o_copy(q).wait()
     w_copy.wait()
 
 
-def multiply(left_ref, right_ref, out_ref):
+def finish(left_ref, right_ref, part_ref, out_ref):
+    kept = part_ref.shape[0]
+    out_ref[:kept] = part_ref[...]
     total = jnp.dot(left_ref[...], right_ref[...], preferred_element_type=jnp.float32)
-    out_ref[...] = total.astype(out_ref.dtype)
+    out_ref[kept:] = total.astype(out_ref.dtype)
 
 
 def body(integrals, amplitudes, screen, next_owner):
@@ -292,19 +316,21 @@
     tiles = row_count // TILE
     n_raw = PAIR
     late = row_count - n_raw * TILE
+    kept = row_count - PAIR * TILE
     last = n_col - 1
     dma = pltpu.SemaphoreType.DMA
     vmem = pl.BlockSpec(memory_space=pltpu.VMEM)
     smem = pl.BlockSpec(memory_space=pltpu.SMEM)
     bf16 = jnp.bfloat16
-    gathered, screened = pl.pallas_call(
+    gathered, screened, part = pl.pallas_call(
         functools.partial(kernel, n_row, n_col, n_raw),
         out_shape=[
-            jax.ShapeDtypeStruct((row_count, n_col * depth), bf16),
+            jax.ShapeDtypeStruct((PAIR * TILE, n_col * depth), bf16),
             jax.ShapeDtypeStruct((n_row * TILE, width), bf16),
+            jax.ShapeDtypeStruct((kept, width), bf16),
         ],
         in_specs=[vmem, vmem, smem, smem],
-        out_specs=[pl.BlockSpec(memory_space=pl.ANY)] * 2,
+        out_specs=[pl.BlockSpec(memory_space=pl.ANY)] * 3,
         scratch_shapes=[
             pltpu.VMEM((n_col, row_count, depth), bf16),
             pltpu.VMEM((bits, late, depth), bf16),
@@ -312,6 +338,7 @@
             pltpu.VMEM((bits, n_col, n_raw * TILE, depth), bf16),
             pltpu.VMEM((n_row, CAP * TILE + 32, TILE), bf16),
             pltpu.VMEM((n_row * TILE, width), bf16),
+            pltpu.VMEM((kept, width), bf16),
             dma((tiles // PAIR, last)),
             dma((tiles // PAIR, last)),
             dma((tiles // PAIR, last)),
@@ -322,8 +349,9 @@
             dma((n_raw, bits)),
             dma((bits,)),
             dma((bits,)),
-            dma((tiles, n_col)),
+            dma((n_col,)),
             dma((1,)),
+            dma((tiles // PAIR - 1,)),
         ],
         compiler_params=pltpu.CompilerParams(
             collective_id=0, has_side_effects=True, vmem_limit_bytes=56 * 1024 * 1024
@@ -331,16 +359,16 @@
     )(integrals, amplitudes, screen, next_owner)
     wide = 2 * TILE
     return pl.pallas_call(
-        multiply,
+        finish,
         out_shape=jax.ShapeDtypeStruct((row_count, width), bf16),
         grid=(width // wide,),
         in_specs=[
             pl.BlockSpec(gathered.shape, lambda n: (0, 0)),
             pl.BlockSpec((screened.shape[0], wide), lambda n: (0, n)),
+            pl.BlockSpec((kept, wide), lambda n: (0, n)),
         ],
         out_specs=pl.BlockSpec((row_count, wide), lambda n: (0, n)),
-        compiler_params=pltpu.CompilerParams(vmem_limit_bytes=48 * 1024 * 1024),
-    )(gathered, screened)
+    )(gathered, screened, part)
 
 
 def solution(mesh):

time: 61 us -> 61.4 us (level)
  Pallas kernels: 57.4 us -> 61.2 us
  local copies, waits for them, and re-layouts: 3.47 us -> 0 us
    unnamed x4 -> x0, local copies, waits for them, and re-layouts: 3.47 us -> none
    pallas_call x1, Pallas kernels: 52 us -> 54.5 us  [body(): pl.pallas_call(functools.partial(kernel, n_row, n_col, n_raw), out_shape=...]
    pallas_call x1, Pallas kernels: 5.38 us -> 6.64 us  [body(): pl.pallas_call(finish, out_shape=jax.ShapeDtypeStruct((row_count, width),...]
where the time goes in v6:
time: 61.4 us; the launch traced here: 61.2 us
  Pallas kernels  61.2 us (100%)
    pallas_call x1, Pallas kernels, body(): pl.pallas_call(functools.partial(kernel, n_row, n_col, n_raw), out_shape=...  54.5 us
    pallas_call x1, Pallas kernels, body(): pl.pallas_call(finish, out_shape=jax.ShapeDtypeStruct((row_count, width),...  6.64 us

profile of v6, /device:TPU:0, one launch (start us, length us, event | category | flops | bytes accessed | tf_op | source)
XLA Modules:
  0.0 61.2 jit_solution(4996680688011496194)
XLA Ops:
  0.0 54.5 %shard_map.46 = (bf16[256,1024]{1,0:T(8,128)(2,1)}, bf16[1024,1536]{1,0:T(8,128)(2,1)}, bf16[768,1536]{1,0:T(8,128)(2,1)}) custom-call(bf16[1024,256]{1,0:T(8,128)(2,1)} %a_ref.1, bf16[128,1536]{1,0:T(8,128)(2,1)} %amp_ref.1, s32[1,12]{1,0:T(1,128)} %scr_ref.1, s32[64]{0:T(128)} %own_ref.1), custom_call_target="tpu_custom_call" | custom-call | tf_op jit(solution)/shard_map/pallas_call | solution.py:325
  54.5 6.6 %shard_map.47 = bf16[1024,1536]{1,0:T(8,128)(2,1)} custom-call(bf16[256,1024]{1,0:T(8,128)(2,1)} %get-tuple-element.8.left_ref, bf16[1024,1536]{1,0:T(8,128)(2,1)} %get-tuple-element.9.right_ref, bf16[768,1536]{1,0:T(8,128)(2,1)} %get-tuple-element.10.part_ref), custom_call_target="tpu_custom_call" | custom-call | tf_op jit(solution)/shard_map/pallas_call | solution.py:361

commit v7 on v6

--- a/solution.py
+++ b/solution.py
@@ -15,9 +15,9 @@
 
 def kernel(
     n_row, n_col, n_raw,
-    a_ref, amp_ref, scr_ref, own_ref, g_out, w_out, part_out,
-    G, X, F, RX, AG, W, O,
-    zr_send, zr_recv, zl_send, zl_recv, p_send, p_recv, r_send, r_recv, a_send, a_recv, g_sem, w_sem, o_sem,
+    a_ref, amp_ref, scr_ref, own_ref, g_out, W, O,
+    G, X, F, RX, AG,
+    zr_send, zr_recv, zl_send, zl_recv, p_send, p_recv, r_send, r_recv, a_send, a_recv,
 ):
     p = lax.axis_index("row")
     c = lax.axis_index("col")
@@ -200,17 +200,10 @@
     wide = 2 * TILE
     kept = tiles // PAIR - 1
 
-    def g_copy(k):
-        at = pl.ds(kept * PAIR * TILE, PAIR * TILE)
-        return pltpu.make_async_copy(G.at[k, at], g_out.at[:, pl.ds(k * depth, depth)], g_sem.at[k])
-
     def put(q):
+        at = pl.ds(q * PAIR * TILE, PAIR * TILE)
         for k in range(n_col):
-            g_copy(k).start()
-
-    def o_copy(q):
-        at = pl.ds(q * PAIR * TILE, PAIR * TILE)
-        return pltpu.make_async_copy(O.at[at], part_out.at[at], o_sem.at[q])
+            g_out[:, k * depth:(k + 1) * depth] = G[k, at]
 
     def compute(q):
         at = pl.ds(q * PAIR * TILE, PAIR * TILE)
@@ -227,9 +220,6 @@
             return carry
 
         lax.fori_loop(0, amp_ref.shape[1] // wide, step, 0)
-        o_copy(q).start()
-
-    w_copy = pltpu.make_async_copy(W, w_out, w_sem.at[0])
 
     last = n_col - 1
     pairs, raw_pairs = tiles // PAIR, n_raw // PAIR
@@ -251,7 +241,6 @@
             a_copy(b).start()
         else:
             expand()
-            w_copy.start()
 
     def own(q):
         if q >= raw_pairs:
@@ -272,7 +261,7 @@
             if q == kept:
                 at_place(4.4 + 1.5 * j + shift, put, q)
             else:
-                at_place(5.35 + 1.6 * j + shift, compute, q)
+                at_place(6.95 + 1.5 * (kept - raw_pairs - 2) + 0.01 * j + shift, compute, q)
         for h in range(1, last):
             if q < raw_pairs:
                 at_place(0.75 + 0.95 * (h - 1), z_hop, q, h)
@@ -294,18 +283,24 @@
             z_edges(q, h, lambda copy: copy.wait_send())
     for b in range(bits):
         a_copy(b).wait_send()
-    for k in range(n_col):
-        g_copy(k).wait()
-    for q in range(kept):
-        o_copy(q).wait()
-    w_copy.wait()
-
-
-def finish(left_ref, right_ref, part_ref, out_ref):
-    kept = part_ref.shape[0]
-    out_ref[:kept] = part_ref[...]
-    total = jnp.dot(left_ref[...], right_ref[...], preferred_element_type=jnp.float32)
-    out_ref[kept:] = total.astype(out_ref.dtype)
+
+def finish(left_ref, right_ref, part_ref, out_ref, held, sem):
+    kept, width = part_ref.shape
+    wide = 2 * TILE
+    carry = pltpu.make_async_copy(part_ref, out_ref.at[pl.ds(0, kept)], sem.at[0])
+    carry.start()
+
+    def step(n, carried):
+        cols = pl.ds(pl.multiple_of(n * wide, wide), wide)
+        total = jnp.dot(left_ref[...], right_ref[:, cols], preferred_element_type=jnp.float32)
+        held[:, cols] = total.astype(held.dtype)
+        return carried
+
+    lax.fori_loop(0, width // wide, step, 0)
+    rest = pltpu.make_async_copy(held, out_ref.at[pl.ds(kept, held.shape[0])], sem.at[1])
+    rest.start()
+    carry.wait()
+    rest.wait()
 
 
 def body(integrals, amplitudes, screen, next_owner):
@@ -318,6 +313,8 @@
     late = row_count - n_raw * TILE
     kept = row_count - PAIR * TILE
     last = n_col - 1
+    held = 2 * (PAIR * TILE * n_col * depth + n_row * TILE * width + kept * width)
+    room = 63 * 1024 * 1024 + 512 * 1024 - held
     dma = pltpu.SemaphoreType.DMA
     vmem = pl.BlockSpec(memory_space=pltpu.VMEM)
     smem = pl.BlockSpec(memory_space=pltpu.SMEM)
@@ -325,20 +322,18 @@
     gathered, screened, part = pl.pallas_call(
         functools.partial(kernel, n_row, n_col, n_raw),
         out_shape=[
-            jax.ShapeDtypeStruct((PAIR * TILE, n_col * depth), bf16),
-            jax.ShapeDtypeStruct((n_row * TILE, width), bf16),
-            jax.ShapeDtypeStruct((kept, width), bf16),
+            pltpu.VMEM((PAIR * TILE, n_col * depth), bf16),
+            pltpu.VMEM((n_row * TILE, width), bf16),
+            pltpu.VMEM((kept, width), bf16),
         ],
         in_specs=[vmem, vmem, smem, smem],
-        out_specs=[pl.BlockSpec(memory_space=pl.ANY)] * 3,
+        out_specs=[vmem] * 3,
         scratch_shapes=[
             pltpu.VMEM((n_col, row_count, depth), bf16),
             pltpu.VMEM((bits, late, depth), bf16),
             pltpu.VMEM((n_col, n_raw * TILE, depth), bf16),
             pltpu.VMEM((bits, n_col, n_raw * TILE, depth), bf16),
             pltpu.VMEM((n_row, CAP * TILE + 32, TILE), bf16),
-            pltpu.VMEM((n_row * TILE, width), bf16),
-            pltpu.VMEM((kept, width), bf16),
             dma((tiles // PAIR, last)),
             dma((tiles // PAIR, last)),
             dma((tiles // PAIR, last)),
@@ -349,25 +344,18 @@
             dma((n_raw, bits)),
             dma((bits,)),
             dma((bits,)),
-            dma((n_col,)),
-            dma((1,)),
-            dma((tiles // PAIR - 1,)),
         ],
         compiler_params=pltpu.CompilerParams(
-            collective_id=0, has_side_effects=True, vmem_limit_bytes=56 * 1024 * 1024
+            collective_id=0, has_side_effects=True, vmem_limit_bytes=room
         ),
     )(integrals, amplitudes, screen, next_owner)
-    wide = 2 * TILE
     return pl.pallas_call(
         finish,
         out_shape=jax.ShapeDtypeStruct((row_count, width), bf16),
-        grid=(width // wide,),
-        in_specs=[
-            pl.BlockSpec(gathered.shape, lambda n: (0, 0)),
-            pl.BlockSpec((screened.shape[0], wide), lambda n: (0, n)),
-            pl.BlockSpec((kept, wide), lambda n: (0, n)),
-        ],
-        out_specs=pl.BlockSpec((row_count, wide), lambda n: (0, n)),
+        in_specs=[vmem] * 3,
+        out_specs=pl.BlockSpec(memory_space=pl.ANY),
+        scratch_shapes=[pltpu.VMEM((row_count - kept, width), bf16), dma((2,))],
+        compiler_params=pltpu.CompilerParams(vmem_limit_bytes=24 * 1024 * 1024),
     )(gathered, screened, part)
 
 

time: 61.4 us -> 58.2 us (0.948)
  Pallas kernels: 61.2 us -> 58 us
    pallas_call x1, Pallas kernels: 6.64 us -> 2.74 us  [body(): pl.pallas_call(finish, out_shape=jax.ShapeDtypeStruct((row_count, width),...]
    pallas_call x1, Pallas kernels: 54.5 us -> 55.3 us  [body(): pl.pallas_call(functools.partial(kernel, n_row, n_col, n_raw), out_shape=...]
where the time goes in v7:
time: 58.2 us; the launch traced here: 58 us
  Pallas kernels  58 us (100%)
    pallas_call x1, Pallas kernels, body(): pl.pallas_call(functools.partial(kernel, n_row, n_col, n_raw), out_shape=...  55.3 us
    pallas_call x1, Pallas kernels, body(): pl.pallas_call(finish, out_shape=jax.ShapeDtypeStruct((row_count, width),...  2.74 us

profile of v7, /device:TPU:0, one launch (start us, length us, event | category | flops | bytes accessed | tf_op | source)
XLA Modules:
  0.0 58.0 jit_solution(2217065604779079172)
XLA Ops:
  0.0 55.3 %shard_map.46 = (bf16[256,1024]{1,0:T(8,128)(2,1)S(1)}, bf16[1024,1536]{1,0:T(8,128)(2,1)S(1)}, bf16[768,1536]{1,0:T(8,128)(2,1)S(1)}) custom-call(bf16[1024,256]{1,0:T(8,128)(2,1)} %a_ref.1, bf16[128,1536]{1,0:T(8,128)(2,1)} %amp_ref.1, s32[1,12]{1,0:T(1,128)} %scr_ref.1, s32[64]{0:T(128)} %own_ref.1), custom_call_target="tpu_custom_call" | custom-call | tf_op jit(solution)/shard_map/pallas_call | solution.py:322
  55.3 2.7 %shard_map.47 = bf16[1024,1536]{1,0:T(8,128)(2,1)} custom-call(bf16[256,1024]{1,0:T(8,128)(2,1)S(1)} %get-tuple-element.8.left_ref, bf16[1024,1536]{1,0:T(8,128)(2,1)S(1)} %get-tuple-element.9.right_ref, bf16[768,1536]{1,0:T(8,128)(2,1)S(1)} %get-tuple-element.10.part_ref), custom_call_target="tpu_custom_call" | custom-call | tf_op jit(solution)/shard_map/pallas_call | solution.py:352

commit v8 on v7

--- a/solution.py
+++ b/solution.py
@@ -10,6 +10,7 @@
 TILE = 128
 CAP = 2
 PAIR = 2
+LEFT = 2
 MESH = pl.DeviceIdType.MESH
 
 
@@ -198,12 +199,13 @@
     depth = a_ref.shape[1]
 
     wide = 2 * TILE
-    kept = tiles // PAIR - 1
+    kept = tiles // PAIR - LEFT
 
     def put(q):
         at = pl.ds(q * PAIR * TILE, PAIR * TILE)
+        to = pl.ds((q - kept) * PAIR * TILE, PAIR * TILE)
         for k in range(n_col):
-            g_out[:, k * depth:(k + 1) * depth] = G[k, at]
+            g_out[to, k * depth:(k + 1) * depth] = G[k, at]
 
     def compute(q):
         at = pl.ds(q * PAIR * TILE, PAIR * TILE)
@@ -247,6 +249,13 @@
             for s in pair(q):
                 p_stage(s, bits)
         z_hop(q, 0)
+
+    def compute_if(q, at_end):
+        ends = (c == 0) | (c == n_col - 1)
+
+        @pl.when(ends if at_end else jnp.logical_not(ends))
+        def _():
+            compute(q)
 
     shift = 0.6 * (bits - 3)
     for q in range(pairs):
@@ -258,10 +267,11 @@
         else:
             at_place((1.6 if j == 0 else 1.0 + 1.2 * j) + shift, own, q)
             at_place(4.4 + 1.5 * j + shift, z_wait, q, last - 1)
-            if q == kept:
+            if q >= kept:
                 at_place(4.4 + 1.5 * j + shift, put, q)
             else:
-                at_place(6.95 + 1.5 * (kept - raw_pairs - 2) + 0.01 * j + shift, compute, q)
+                at_place(4.45 + 1.5 * j + shift, compute_if, q, True)
+                at_place(6.95 + 1.5 * (pairs - raw_pairs - 3) + 0.01 * j + shift, compute_if, q, False)
         for h in range(1, last):
             if q < raw_pairs:
                 at_place(0.75 + 0.95 * (h - 1), z_hop, q, h)
@@ -290,17 +300,24 @@
     carry = pltpu.make_async_copy(part_ref, out_ref.at[pl.ds(0, kept)], sem.at[0])
     carry.start()
 
-    def step(n, carried):
-        cols = pl.ds(pl.multiple_of(n * wide, wide), wide)
-        total = jnp.dot(left_ref[...], right_ref[:, cols], preferred_element_type=jnp.float32)
-        held[:, cols] = total.astype(held.dtype)
-        return carried
-
-    lax.fori_loop(0, width // wide, step, 0)
-    rest = pltpu.make_async_copy(held, out_ref.at[pl.ds(kept, held.shape[0])], sem.at[1])
-    rest.start()
+    size = PAIR * TILE
+    rests = []
+    for q in range(LEFT):
+        at = pl.ds(q * size, size)
+
+        def step(n, carried):
+            cols = pl.ds(pl.multiple_of(n * wide, wide), wide)
+            total = jnp.dot(left_ref[at], right_ref[:, cols], preferred_element_type=jnp.float32)
+            held[at, cols] = total.astype(held.dtype)
+            return carried
+
+        lax.fori_loop(0, width // wide, step, 0)
+        rest = pltpu.make_async_copy(held.at[at], out_ref.at[pl.ds(kept + q * size, size)], sem.at[1 + q])
+        rest.start()
+        rests.append(rest)
     carry.wait()
-    rest.wait()
+    for rest in rests:
+        rest.wait()
 
 
 def body(integrals, amplitudes, screen, next_owner):
@@ -311,9 +328,9 @@
     tiles = row_count // TILE
     n_raw = PAIR
     late = row_count - n_raw * TILE
-    kept = row_count - PAIR * TILE
+    kept = row_count - LEFT * PAIR * TILE
     last = n_col - 1
-    held = 2 * (PAIR * TILE * n_col * depth + n_row * TILE * width + kept * width)
+    held = 2 * (LEFT * PAIR * TILE * n_col * depth + n_row * TILE * width + kept * width)
     room = 63 * 1024 * 1024 + 512 * 1024 - held
     dma = pltpu.SemaphoreType.DMA
     vmem = pl.BlockSpec(memory_space=pltpu.VMEM)
@@ -322,7 +339,7 @@
     gathered, screened, part = pl.pallas_call(
         functools.partial(kernel, n_row, n_col, n_raw),
         out_shape=[
-            pltpu.VMEM((PAIR * TILE, n_col * depth), bf16),
+            pltpu.VMEM((LEFT * PAIR * TILE, n_col * depth), bf16),
             pltpu.VMEM((n_row * TILE, width), bf16),
             pltpu.VMEM((kept, width), bf16),
         ],
@@ -354,7 +371,7 @@
         out_shape=jax.ShapeDtypeStruct((row_count, width), bf16),
         in_specs=[vmem] * 3,
         out_specs=pl.BlockSpec(memory_space=pl.ANY),
-        scratch_shapes=[pltpu.VMEM((row_count - kept, width), bf16), dma((2,))],
+        scratch_shapes=[pltpu.VMEM((row_count - kept, width), bf16), dma((1 + LEFT,))],
         compiler_params=pltpu.CompilerParams(vmem_limit_bytes=24 * 1024 * 1024),
     )(gathered, screened, part)
 

time: 58.2 us -> 56.4 us (0.969)
  Pallas kernels: 58 us -> 56.3 us
    pallas_call x1, Pallas kernels: 55.3 us -> 51.7 us  [body(): pl.pallas_call(functools.partial(kernel, n_row, n_col, n_raw), out_shape=...]
    pallas_call x1, Pallas kernels: 2.74 us -> 4.6 us  [body(): pl.pallas_call(finish, out_shape=jax.ShapeDtypeStruct((row_count, width),...]
where the time goes in v8:
time: 56.4 us; the launch traced here: 56.3 us
  Pallas kernels  56.3 us (100%)
    pallas_call x1, Pallas kernels, body(): pl.pallas_call(functools.partial(kernel, n_row, n_col, n_raw), out_shape=...  51.7 us
    pallas_call x1, Pallas kernels, body(): pl.pallas_call(finish, out_shape=jax.ShapeDtypeStruct((row_count, width),...  4.6 us

profile of v8, /device:TPU:0, one launch (start us, length us, event | category | flops | bytes accessed | tf_op | source)
XLA Modules:
  0.0 56.3 jit_solution(4588928519331387804)
XLA Ops:
  0.0 51.7 %shard_map.46 = (bf16[512,1024]{1,0:T(8,128)(2,1)S(1)}, bf16[1024,1536]{1,0:T(8,128)(2,1)S(1)}, bf16[512,1536]{1,0:T(8,128)(2,1)S(1)}) custom-call(bf16[1024,256]{1,0:T(8,128)(2,1)} %a_ref.1, bf16[128,1536]{1,0:T(8,128)(2,1)} %amp_ref.1, s32[1,12]{1,0:T(1,128)} %scr_ref.1, s32[64]{0:T(128)} %own_ref.1), custom_call_target="tpu_custom_call" | custom-call | tf_op jit(solution)/shard_map/pallas_call | solution.py:339
  51.7 4.6 %shard_map.47 = bf16[1024,1536]{1,0:T(8,128)(2,1)} custom-call(bf16[512,1024]{1,0:T(8,128)(2,1)S(1)} %get-tuple-element.8.left_ref, bf16[1024,1536]{1,0:T(8,128)(2,1)S(1)} %get-tuple-element.9.right_ref, bf16[512,1536]{1,0:T(8,128)(2,1)S(1)} %get-tuple-element.10.part_ref), custom_call_target="tpu_custom_call" | custom-call | tf_op jit(solution)/shard_map/pallas_call | solution.py:369

commit v9 on v8

--- a/solution.py
+++ b/solution.py
@@ -10,7 +10,7 @@
 TILE = 128
 CAP = 2
 PAIR = 2
-LEFT = 2
+LEFT = 1
 MESH = pl.DeviceIdType.MESH
 
 

time: 56.4 us -> 56.3 us (level)
    pallas_call x1, Pallas kernels: 4.6 us -> 2.75 us  [body(): pl.pallas_call(finish, out_shape=jax.ShapeDtypeStruct((row_count, width),...]
    pallas_call x1, Pallas kernels: 51.7 us -> 53.4 us  [body(): pl.pallas_call(functools.partial(kernel, n_row, n_col, n_raw), out_shape=...]
where the time goes in v9:
time: 56.3 us; the launch traced here: 56.2 us
  Pallas kernels  56.2 us (100%)
    pallas_call x1, Pallas kernels, body(): pl.pallas_call(functools.partial(kernel, n_row, n_col, n_raw), out_shape=...  53.4 us
    pallas_call x1, Pallas kernels, body(): pl.pallas_call(finish, out_shape=jax.ShapeDtypeStruct((row_count, width),...  2.75 us

profile of v9, /device:TPU:0, one launch (start us, length us, event | category | flops | bytes accessed | tf_op | source)
XLA Modules:
  0.0 56.2 jit_solution(14483504529682878789)
XLA Ops:
  0.0 53.4 %shard_map.46 = (bf16[256,1024]{1,0:T(8,128)(2,1)S(1)}, bf16[1024,1536]{1,0:T(8,128)(2,1)S(1)}, bf16[768,1536]{1,0:T(8,128)(2,1)S(1)}) custom-call(bf16[1024,256]{1,0:T(8,128)(2,1)} %a_ref.1, bf16[128,1536]{1,0:T(8,128)(2,1)} %amp_ref.1, s32[1,12]{1,0:T(1,128)} %scr_ref.1, s32[64]{0:T(128)} %own_ref.1), custom_call_target="tpu_custom_call" | custom-call | tf_op jit(solution)/shard_map/pallas_call | solution.py:339
  53.4 2.8 %shard_map.47 = bf16[1024,1536]{1,0:T(8,128)(2,1)} custom-call(bf16[256,1024]{1,0:T(8,128)(2,1)S(1)} %get-tuple-element.8.left_ref, bf16[1024,1536]{1,0:T(8,128)(2,1)S(1)} %get-tuple-element.9.right_ref, bf16[768,1536]{1,0:T(8,128)(2,1)S(1)} %get-tuple-element.10.part_ref), custom_call_target="tpu_custom_call" | custom-call | tf_op jit(solution)/shard_map/pallas_call | solution.py:369

commit v10 on v9

--- a/solution.py
+++ b/solution.py
@@ -263,7 +263,8 @@
         if q < raw_pairs:
             at_place(0.0, own, q)
             at_place(2.6, z_wait, q, last - 1)
-            at_place(6.9 + 1.7 * (bits - 3) + shift, compute, q)
+            at_place(2.65 + 1.37 * (bits - 1) + 0.42, compute_if, q, True)
+            at_place(6.9 + 1.7 * (bits - 3) + shift, compute_if, q, False)
         else:
             at_place((1.6 if j == 0 else 1.0 + 1.2 * j) + shift, own, q)
             at_place(4.4 + 1.5 * j + shift, z_wait, q, last - 1)
@@ -280,7 +281,7 @@
         for s in pair(q):
             for i in range(bits + 1):
                 if q < raw_pairs:
-                    at_place(2.65 + 1.7 * i - (0.9 if i == bits else 0.0), r_stage, s, i)
+                    at_place(2.65 + 1.37 * i - (0.97 if i == bits else 0.0), r_stage, s, i)
                 elif i < bits:
                     at_place(0.05 + 0.6 * i + 0.65 * j, p_stage, s, i)
     for b in range(bits + 1):

time: 56.3 us -> 53.8 us (0.956)
  Pallas kernels: 56.2 us -> 53.7 us
    pallas_call x1, Pallas kernels: 53.4 us -> 51 us  [body(): pl.pallas_call(functools.partial(kernel, n_row, n_col, n_raw), out_shape=...]
where the time goes in v10:
time: 53.8 us; the launch traced here: 53.7 us
  Pallas kernels  53.7 us (100%)
    pallas_call x1, Pallas kernels, body(): pl.pallas_call(functools.partial(kernel, n_row, n_col, n_raw), out_shape=...  51 us
    pallas_call x1, Pallas kernels, body(): pl.pallas_call(finish, out_shape=jax.ShapeDtypeStruct((row_count, width),...  2.74 us

profile of v10, /device:TPU:0, one launch (start us, length us, event | category | flops | bytes accessed | tf_op | source)
XLA Modules:
  0.0 53.7 jit_solution(3965210224582037915)
XLA Ops:
  0.0 51.0 %shard_map.46 = (bf16[256,1024]{1,0:T(8,128)(2,1)S(1)}, bf16[1024,1536]{1,0:T(8,128)(2,1)S(1)}, bf16[768,1536]{1,0:T(8,128)(2,1)S(1)}) custom-call(bf16[1024,256]{1,0:T(8,128)(2,1)} %a_ref.1, bf16[128,1536]{1,0:T(8,128)(2,1)} %amp_ref.1, s32[1,12]{1,0:T(1,128)} %scr_ref.1, s32[64]{0:T(128)} %own_ref.1), custom_call_target="tpu_custom_call" | custom-call | tf_op jit(solution)/shard_map/pallas_call | solution.py:340
  51.0 2.7 %shard_map.47 = bf16[1024,1536]{1,0:T(8,128)(2,1)} custom-call(bf16[256,1024]{1,0:T(8,128)(2,1)S(1)} %get-tuple-element.8.left_ref, bf16[1024,1536]{1,0:T(8,128)(2,1)S(1)} %get-tuple-element.9.right_ref, bf16[768,1536]{1,0:T(8,128)(2,1)S(1)} %get-tuple-element.10.part_ref), custom_call_target="tpu_custom_call" | custom-call | tf_op jit(solution)/shard_map/pallas_call | solution.py:370
